TPU v7x, 32 devices: a whole 2x2x4 slice. The times are simulated.
32 devices in a mesh: groups: 2 (over y), scan: 16 (over z, x, core), obj: 1, sub: 1.
Axes of the slice: x: 2, y: 2, z: 4, core: 2. Of those that a mesh axis runs over, the one named last changes fastest.
Arguments:
- object_field: float32 [2, 8192, 512], P(None, ('groups', 'scan'), 'obj'), parts along dimension 1, may hold values from -3 to 3
- probe_field: float32 [4, 256, 256], P('groups'), parts along dimension 0, may hold values from -3 to 3
- intensities: float32 [2, 1, 96, 256, 256], P(('groups', 'obj'), 'sub', 'scan'), parts along dimension 0, may hold values from 0.05 to 0.5
- positions: int32 [2, 1, 96, 2], P(('groups', 'obj'), 'sub', 'scan'), parts along dimension 0, may hold values from 0 to 3839, as said below
- live_counts: int32 [2, 1, 16], P(('groups', 'obj'), 'sub', 'scan'), parts along dimension 0, may hold values from 5 to 6, as said below
Outputs:
- object_grad: float32 [2, 8192, 512], P(None, ('groups', 'scan'), 'obj'), parts along dimension 1
- probe_grad: float32 [4, 256, 256], P('groups'), parts along dimension 0
There are 2 independent parts, one for each index of `groups`. A program takes and returns all parts, laid end to end along the dimension named above; each array names one. Nothing has to cross between parts.
Inputs may be any that keep to these rules, and one draw needn't show every extreme that they name: `positions`: row r lies in band r // 256; the bands of the 6 slots of one device differ pairwise by 2 or more, none exceeds 16 - 2, and slots run in increasing or decreasing band order. Column c of a pattern in stripe o lies from o * 512 to o * 512 + 256. The live slots of a device are its first live_counts ones.
All inputs are finite; a program needn't handle non-finite values.
Results may differ from a plain program's by a relative error of at most 0.0033.
The roundings to bfloat16 on the way count: a program that leaves them out, or rounds other values in their place, can miss the bound.
Values may be sent and summed in bfloat16 or wider, within the bound.
A program may use at most 64 MiB of HBM per device.

v0:
```python
import math

import jax
import jax.numpy as jnp
from jax import lax
from jax.sharding import PartitionSpec as P


def dft_tables(pixels):
    counter = jnp.arange(pixels, dtype=jnp.int32)
    product = counter[:, None] * counter[None, :] % pixels
    angle = product.astype(jnp.float32) * (2.0 * math.pi / pixels)
    factor = 1.0 / math.sqrt(pixels)
    return (jnp.cos(angle) * factor, jnp.sin(angle) * factor)


def transform(real_part, imag_part, cosine_table, signed_sine):
    highest = lax.Precision.HIGHEST
    left_real = jnp.einsum("kn,pnm->pkm", cosine_table, real_part, precision=highest) - jnp.einsum(
        "kn,pnm->pkm", signed_sine, imag_part, precision=highest
    )
    left_imag = jnp.einsum("kn,pnm->pkm", cosine_table, imag_part, precision=highest) + jnp.einsum(
        "kn,pnm->pkm", signed_sine, real_part, precision=highest
    )
    out_real = jnp.einsum("pkn,nm->pkm", left_real, cosine_table, precision=highest) - jnp.einsum(
        "pkn,nm->pkm", left_imag, signed_sine, precision=highest
    )
    out_imag = jnp.einsum("pkn,nm->pkm", left_imag, cosine_table, precision=highest) + jnp.einsum(
        "pkn,nm->pkm", left_real, signed_sine, precision=highest
    )
    return (out_real, out_imag)


def far_side(real_object, imag_object, measured, living, probe_field, cosine_table, sine_table):
    probe_real = probe_field[0]
    probe_imag = probe_field[1]
    wave_real = probe_real * real_object - probe_imag * imag_object
    wave_imag = probe_real * imag_object + probe_imag * real_object
    far_real, far_imag = transform(wave_real, wave_imag, cosine_table, -sine_table)
    misfit = far_real * far_real + far_imag * far_imag - measured
    back_real, back_imag = transform(misfit * far_real, misfit * far_imag, cosine_table, sine_table)
    back_real = back_real * living[:, None, None]
    back_imag = back_imag * living[:, None, None]
    step_low = jnp.stack(
        [
            probe_real * back_real + probe_imag * back_imag,
            probe_real * back_imag - probe_imag * back_real,
        ],
        axis=1,
    ).astype(jnp.bfloat16)
    probe_part = jnp.stack(
        [
            jnp.sum(real_object * back_real + imag_object * back_imag, axis=0),
            jnp.sum(real_object * back_imag - imag_object * back_real, axis=0),
        ]
    )
    return (step_low, probe_part)


def on_device(object_field, probe_field, intensities, positions, live_counts):
    pixels = probe_field.shape[1]
    stripe = object_field.shape[2]
    patterns_here = positions.shape[2]
    scan_count = lax.axis_size("scan")
    owner_index = lax.axis_index("scan")
    column_base = lax.axis_index("obj") * stripe
    gathered_places, gathered_counts = (
        lax.all_gather(positions, "scan", axis=2, tiled=True),
        lax.all_gather(live_counts, "scan", axis=2, tiled=True),
    )
    every_place = gathered_places.reshape(scan_count, patterns_here, 2)
    every_count = gathered_counts.reshape(scan_count)
    slot_numbers = jnp.arange(patterns_here, dtype=jnp.int32)
    peer_live = slot_numbers[None, :] < every_count[:, None]
    peer_band = every_place[..., 0] // pixels
    peer_rows = every_place[..., 0] - owner_index * pixels
    peer_cols = every_place[..., 1] - column_base
    own_place = positions.reshape(patterns_here, 2)
    own_band = own_place[:, 0] // pixels
    own_live = slot_numbers < live_counts.reshape(())
    owners = jnp.arange(scan_count, dtype=jnp.int32)
    tile_low = object_field.astype(jnp.bfloat16)
    cosine_table, sine_table = dft_tables(pixels)
    zero_index = jnp.zeros((), jnp.int32)
    own_measured = intensities.reshape(patterns_here, pixels, pixels)
    extended = jnp.pad(tile_low, ((0, 0), (pixels, pixels), (0, 0)))
    matched = peer_live & ((peer_band == owner_index) | (peer_band + 1 == owner_index))
    targets = own_live[:, None] & (
        (own_band[:, None] == owners[None, :]) | (own_band[:, None] + 1 == owners[None, :])
    )
    row_offsets = jnp.sum(jnp.where(matched, peer_rows, 0), axis=1) + pixels
    col_offsets = jnp.sum(jnp.where(matched, peer_cols, 0), axis=1)
    serving = jnp.any(matched, axis=1)

    def cut_window(row_start, col_start):
        return lax.dynamic_slice(extended, (zero_index, row_start, col_start), (2, pixels, pixels))

    windows = jax.vmap(cut_window)(row_offsets, col_offsets)
    windows = jnp.where(serving[:, None, None, None], windows, jnp.zeros_like(windows))
    received = lax.all_to_all(windows, "scan", split_axis=0, concat_axis=0, tiled=True)
    target_weights = targets.astype(jnp.bfloat16)
    object_patch = jnp.einsum(
        "js,scab->jcab", target_weights, received, preferred_element_type=jnp.float32
    )
    step_low, probe_part = far_side(
        object_patch[:, 0],
        object_patch[:, 1],
        own_measured,
        own_live.astype(jnp.float32),
        probe_field,
        cosine_table,
        sine_table,
    )
    returned = jnp.einsum(
        "js,jcab->scab", target_weights, step_low, preferred_element_type=jnp.float32
    ).astype(jnp.bfloat16)
    incoming = lax.all_to_all(returned, "scan", split_axis=0, concat_axis=0, tiled=True)

    def add_piece(source, accumulated):
        start = (zero_index, row_offsets[source], col_offsets[source])
        current = lax.dynamic_slice(accumulated, start, (2, pixels, pixels))
        piece_value = jnp.where(
            serving[source],
            incoming[source].astype(jnp.float32),
            jnp.zeros((2, pixels, pixels), jnp.float32),
        )
        return lax.dynamic_update_slice(accumulated, current + piece_value, start)

    accumulated = lax.fori_loop(0, scan_count, add_piece, jnp.zeros(extended.shape, jnp.float32))
    tile_grad = accumulated[:, pixels : 2 * pixels, :]
    object_grad = lax.psum(tile_grad, "sub")
    probe_grad = lax.psum(probe_part, ("scan", "obj", "sub"))
    return (object_grad, probe_grad)


def solution(mesh):
    placed = (
        P(None, ("groups", "scan"), "obj"),
        P("groups", None, None),
        P(("groups", "obj"), "sub", "scan", None, None),
        P(("groups", "obj"), "sub", "scan", None),
        P(("groups", "obj"), "sub", "scan"),
    )
    return jax.shard_map(
        on_device,
        mesh=mesh,
        in_specs=placed,
        out_specs=(P(None, ("groups", "scan"), "obj"), P("groups", None, None)),
        check_vma=False,
    )
```

profile of v0, /device:TPU:15, one launch (start us, length us, event | category | flops | bytes accessed | tf_op | source)
XLA Modules:
  0.0 614.7 jit_solution(15022627021345711849)
XLA Ops:
  9.8 7.9 %all-reduce.1 = s32[16]{0:T(128)S(1)} all-reduce(s32[16]{0:T(128)S(1)} %bitcast_dynamic-update-slice_fusion.1), channel_id=1, replica_groups=mesh['groups'=2,'scan'=16,'obj'=1,'sub'=1] {'scan'}, use_global_device_ids=true, to_apply=%add.1 | all-reduce | flops 16 | bytes 128
  18.4 19.8 %all_gather.7 = s32[1,1,96,2]{3,1,0,2:T(1,128)S(1)} all-gather(s32[1,1,6,2]{3,1,0,2:T(1,128)S(1)} %copy.55), channel_id=1, replica_groups=mesh['groups'=2,'scan'=16,'obj'=1,'sub'=1] {'scan'}, dimensions={2}, use_global_device_ids=true | all-gather | bytes 816 | tf_op jit(solution)/shard_map/all_gather | solution.py:68
  40.1 44.2 %while.17 = (s32[]{:T(128)}, bf16[2,768,512]{2,1,0:T(8,128)(2,1)S(1)}, s32[16,3]{0,1:T(4,128)S(1)}, bf16[16,2,256,256]{3,2,1,0:T(8,128)(2,1)}) while((s32[]{:T(128)}, bf16[2,768,512]{2,1,0:T(8,128)(2,1)S(1)}, s32[16,3]{0,1:T(4,128)S(1)}, bf16[16,2,256,256]{3,2,1,0:T(8,128)(2,1)}) %tuple.69), condition=%wide.while_cond.clone, body=%wide.while_body.sunk.clone | while | flops 2 | bytes 525921 | solution.py:96
  84.2 4.5 broadcast_select_fusion
  88.8 7.8 %all-to-all-start = ((bf16[16,2,256,256]{3,2,1,0:T(8,128)(2,1)}), bf16[16,2,256,256]{3,2,1,0:T(8,128)(2,1)}, u32[]{:S(2)}, u32[]{:S(2)}) async-start(bf16[16,2,256,256]{3,2,1,0:T(8,128)(2,1)} %broadcast_select_fusion), calls=%async_computation | async-start | bytes 8388608 | tf_op jit(solution)/shard_map/all_to_all | solution.py:100
  96.7 92.4 %all-to-all-done = bf16[16,2,256,256]{3,2,1,0:T(8,128)(2,1)} async-done(((bf16[16,2,256,256]{3,2,1,0:T(8,128)(2,1)}), bf16[16,2,256,256]{3,2,1,0:T(8,128)(2,1)}, u32[]{:S(2)}, u32[]{:S(2)}) %all-to-all-start) | async-done | bytes 4194336 | tf_op jit(solution)/shard_map/all_to_all | solution.py:100
  189.0 4.6 fusion
  213.1 3.8 fusion.15
  226.8 4.0 fusion.48
  230.7 3.7 convolution_subtract_fusion
  238.1 4.1 fusion.13
  253.3 3.8 fusion.9
  257.1 11.0 %add_reduce_fusion = (f32[256,256]{1,0:T(8,128)S(1)}, f32[256,256]{1,0:T(8,128)S(1)}, bf16[6,1,256,256]{3,0,2,1:T(8,128)(2,1)S(1)}, bf16[6,1,256,256]{3,0,2,1:T(8,128)(2,1)S(1)}) fusion(f32[6,2,256,256]{3,0,2,1:T(8,128)S(1)} %copy-done.1, f32[6]{0:T(128)S(1)} %get-tuple-element.183, f32[6,256,256]{2,1,0:T(8,128)S(1)} %fusion.9, ...), kind=kLoop, calls=%fused_computation.17 | loop fusion | flops 7733248 | bytes 12058648 | tf_op jit(solution)/shard_map/reduce_sum | solution.py:53
  273.3 4.9 all-to-all-start.1
  279.1 96.1 %all-to-all-done.1 = bf16[16,2,256,256]{3,2,1,0:T(8,128)(2,1)} async-done(((bf16[16,2,256,256]{3,2,1,0:T(8,128)(2,1)}), bf16[16,2,256,256]{3,2,1,0:T(8,128)(2,1)}, u32[]{:S(2)}, u32[]{:S(2)}) %all-to-all-start.1) | async-done | bytes 4194336 | tf_op jit(solution)/shard_map/all_to_all | solution.py:117
  377.3 226.2 %while.16 = (s32[]{:T(128)}, f32[2,768,512]{2,1,0:T(8,128)}, s32[16]{0:T(128)S(1)}, s32[16]{0:T(128)S(1)}, pred[16]{0:T(512)(128)(4,1)S(1)}, /*index=5*/bf16[16,2,256,256]{3,2,1,0:T(8,128)(2,1)}) while((s32[]{:T(128)}, f32[2,768,512]{2,1,0:T(8,128)}, s32[16]{0:T(128)S(1)}, s32[16]{0:T(128)S(1)}, pred[16]{0:T(512)(128)(4,1)S(1)}, ...), condition=%wide.region_4.5_spmd.clone, body=%wide.region_3.4_spmd.sunk.clone | while | flops 393224 | bytes 2359480 | solution.py:129
  385.0 6.5 %dynamic_update_slice.9 = f32[2,768,512]{2,1,0:T(8,128)} dynamic-update-slice(f32[2,768,512]{2,1,0:T(8,128)} %get-tuple-element.298, f32[2,256,256]{2,1,0:T(8,128)S(1)} %bitcast_add_fusion.3, s32[]{:T(128)} %constant.94.clone.1..sunk.1, s32[]{:T(128)S(6)} %select_n.215, s32[]{:T(128)S(6)} %select_n.216) | dynamic-update-slice | bytes 1048580 | tf_op jit(solution)/shard_map/while/body/eval_jaxpr/dynamic_update_slice | solution.py:127
  399.3 6.8 %dynamic_update_slice.9 = f32[2,768,512]{2,1,0:T(8,128)} dynamic-update-slice(f32[2,768,512]{2,1,0:T(8,128)} %get-tuple-element.298, f32[2,256,256]{2,1,0:T(8,128)S(1)} %bitcast_add_fusion.3, s32[]{:T(128)} %constant.94.clone.1..sunk.1, s32[]{:T(128)S(6)} %select_n.215, s32[]{:T(128)S(6)} %select_n.216) | dynamic-update-slice | bytes 1048580 | tf_op jit(solution)/shard_map/while/body/eval_jaxpr/dynamic_update_slice | solution.py:127
  413.8 6.8 %dynamic_update_slice.9 = f32[2,768,512]{2,1,0:T(8,128)} dynamic-update-slice(f32[2,768,512]{2,1,0:T(8,128)} %get-tuple-element.298, f32[2,256,256]{2,1,0:T(8,128)S(1)} %bitcast_add_fusion.3, s32[]{:T(128)} %constant.94.clone.1..sunk.1, s32[]{:T(128)S(6)} %select_n.215, s32[]{:T(128)S(6)} %select_n.216) | dynamic-update-slice | bytes 1048580 | tf_op jit(solution)/shard_map/while/body/eval_jaxpr/dynamic_update_slice | solution.py:127
  428.2 5.9 dynamic_update_slice.9
  441.8 6.8 %dynamic_update_slice.9 = f32[2,768,512]{2,1,0:T(8,128)} dynamic-update-slice(f32[2,768,512]{2,1,0:T(8,128)} %get-tuple-element.298, f32[2,256,256]{2,1,0:T(8,128)S(1)} %bitcast_add_fusion.3, s32[]{:T(128)} %constant.94.clone.1..sunk.1, s32[]{:T(128)S(6)} %select_n.215, s32[]{:T(128)S(6)} %select_n.216) | dynamic-update-slice | bytes 1048580 | tf_op jit(solution)/shard_map/while/body/eval_jaxpr/dynamic_update_slice | solution.py:127
  456.3 6.5 %dynamic_update_slice.9 = f32[2,768,512]{2,1,0:T(8,128)} dynamic-update-slice(f32[2,768,512]{2,1,0:T(8,128)} %get-tuple-element.298, f32[2,256,256]{2,1,0:T(8,128)S(1)} %bitcast_add_fusion.3, s32[]{:T(128)} %constant.94.clone.1..sunk.1, s32[]{:T(128)S(6)} %select_n.215, s32[]{:T(128)S(6)} %select_n.216) | dynamic-update-slice | bytes 1048580 | tf_op jit(solution)/shard_map/while/body/eval_jaxpr/dynamic_update_slice | solution.py:127
  470.5 6.5 %dynamic_update_slice.9 = f32[2,768,512]{2,1,0:T(8,128)} dynamic-update-slice(f32[2,768,512]{2,1,0:T(8,128)} %get-tuple-element.298, f32[2,256,256]{2,1,0:T(8,128)S(1)} %bitcast_add_fusion.3, s32[]{:T(128)} %constant.94.clone.1..sunk.1, s32[]{:T(128)S(6)} %select_n.215, s32[]{:T(128)S(6)} %select_n.216) | dynamic-update-slice | bytes 1048580 | tf_op jit(solution)/shard_map/while/body/eval_jaxpr/dynamic_update_slice | solution.py:127
  484.7 6.4 %dynamic_update_slice.9 = f32[2,768,512]{2,1,0:T(8,128)} dynamic-update-slice(f32[2,768,512]{2,1,0:T(8,128)} %get-tuple-element.298, f32[2,256,256]{2,1,0:T(8,128)S(1)} %bitcast_add_fusion.3, s32[]{:T(128)} %constant.94.clone.1..sunk.1, s32[]{:T(128)S(6)} %select_n.215, s32[]{:T(128)S(6)} %select_n.216) | dynamic-update-slice | bytes 1048580 | tf_op jit(solution)/shard_map/while/body/eval_jaxpr/dynamic_update_slice | solution.py:127
  498.9 6.8 %dynamic_update_slice.9 = f32[2,768,512]{2,1,0:T(8,128)} dynamic-update-slice(f32[2,768,512]{2,1,0:T(8,128)} %get-tuple-element.298, f32[2,256,256]{2,1,0:T(8,128)S(1)} %bitcast_add_fusion.3, s32[]{:T(128)} %constant.94.clone.1..sunk.1, s32[]{:T(128)S(6)} %select_n.215, s32[]{:T(128)S(6)} %select_n.216) | dynamic-update-slice | bytes 1048580 | tf_op jit(solution)/shard_map/while/body/eval_jaxpr/dynamic_update_slice | solution.py:127
  513.3 6.1 dynamic_update_slice.9
  527.1 5.9 dynamic_update_slice.9
  540.7 6.6 %dynamic_update_slice.9 = f32[2,768,512]{2,1,0:T(8,128)} dynamic-update-slice(f32[2,768,512]{2,1,0:T(8,128)} %get-tuple-element.298, f32[2,256,256]{2,1,0:T(8,128)S(1)} %bitcast_add_fusion.3, s32[]{:T(128)} %constant.94.clone.1..sunk.1, s32[]{:T(128)S(6)} %select_n.215, s32[]{:T(128)S(6)} %select_n.216) | dynamic-update-slice | bytes 1048580 | tf_op jit(solution)/shard_map/while/body/eval_jaxpr/dynamic_update_slice | solution.py:127
  555.0 6.3 %dynamic_update_slice.9 = f32[2,768,512]{2,1,0:T(8,128)} dynamic-update-slice(f32[2,768,512]{2,1,0:T(8,128)} %get-tuple-element.298, f32[2,256,256]{2,1,0:T(8,128)S(1)} %bitcast_add_fusion.3, s32[]{:T(128)} %constant.94.clone.1..sunk.1, s32[]{:T(128)S(6)} %select_n.215, s32[]{:T(128)S(6)} %select_n.216) | dynamic-update-slice | bytes 1048580 | tf_op jit(solution)/shard_map/while/body/eval_jaxpr/dynamic_update_slice | solution.py:127
  568.9 6.5 %dynamic_update_slice.9 = f32[2,768,512]{2,1,0:T(8,128)} dynamic-update-slice(f32[2,768,512]{2,1,0:T(8,128)} %get-tuple-element.298, f32[2,256,256]{2,1,0:T(8,128)S(1)} %bitcast_add_fusion.3, s32[]{:T(128)} %constant.94.clone.1..sunk.1, s32[]{:T(128)S(6)} %select_n.215, s32[]{:T(128)S(6)} %select_n.216) | dynamic-update-slice | bytes 1048580 | tf_op jit(solution)/shard_map/while/body/eval_jaxpr/dynamic_update_slice | solution.py:127
  583.1 5.9 dynamic_update_slice.9
  596.7 6.8 %dynamic_update_slice.9 = f32[2,768,512]{2,1,0:T(8,128)} dynamic-update-slice(f32[2,768,512]{2,1,0:T(8,128)} %get-tuple-element.298, f32[2,256,256]{2,1,0:T(8,128)S(1)} %bitcast_add_fusion.3, s32[]{:T(128)} %constant.94.clone.1..sunk.1, s32[]{:T(128)S(6)} %select_n.215, s32[]{:T(128)S(6)} %select_n.216) | dynamic-update-slice | bytes 1048580 | tf_op jit(solution)/shard_map/while/body/eval_jaxpr/dynamic_update_slice | solution.py:127
  (172 shorter events, 168.3 us)
Async XLA Ops:
  88.7 7.8 %copy-start.7 = (s32[1,1,6,2]{2,3,1,0:T(2,128)S(1)}, s32[1,1,6,2]{2,3,1,0:T(2,128)}, u32[]{:S(2)}) copy-start(s32[1,1,6,2]{2,3,1,0:T(2,128)} %param.10) | copy-start | bytes 148
  88.8 7.8 %copy-start.6 = (f32[2,256,256]{2,1,0:T(8,128)S(1)}, f32[2,256,256]{2,1,0:T(8,128)}, u32[]{:S(2)}) copy-start(f32[2,256,256]{2,1,0:T(8,128)} %param.8) | copy-start | bytes 1572868
  88.8 100.3 %all-to-all-start = ((bf16[16,2,256,256]{3,2,1,0:T(8,128)(2,1)}), bf16[16,2,256,256]{3,2,1,0:T(8,128)(2,1)}, u32[]{:S(2)}, u32[]{:S(2)}) async-start(bf16[16,2,256,256]{3,2,1,0:T(8,128)(2,1)} %broadcast_select_fusion), calls=%async_computation | async-start | bytes 8388608 | tf_op jit(solution)/shard_map/all_to_all | solution.py:100
  96.6 97.0 %copy-start.4 = (f32[256,256]{1,0:T(8,128)}, f32[256,256]{1,0:T(8,128)S(1)}, u32[]{:S(2)}) copy-start(f32[256,256]{1,0:T(8,128)S(1)} %get-tuple-element.177) | copy-start | bytes 786436
  193.6 3.3 copy-start
  213.1 3.8 copy-start.3
  223.0 3.7 copy-start.2
  249.7 7.4 %copy-start.1 = (f32[6,2,256,256]{3,0,2,1:T(8,128)S(1)}, f32[6,2,256,256]{3,0,2,1:T(8,128)}, u32[]{:S(2)}) copy-start(f32[6,2,256,256]{3,0,2,1:T(8,128)} %copy-done) | copy-start | bytes 9437188
  253.3 3.8 copy-start.5
  273.3 101.9 %all-to-all-start.1 = ((bf16[16,2,256,256]{3,2,1,0:T(8,128)(2,1)}), bf16[16,2,256,256]{3,2,1,0:T(8,128)(2,1)}, u32[]{:S(2)}, u32[]{:S(2)}) async-start(bf16[16,2,256,256]{3,2,1,0:T(8,128)(2,1)} %copy.80), calls=%async_computation.1 | async-start | bytes 8388608 | tf_op jit(solution)/shard_map/all_to_all | solution.py:117
  278.2 327.5 %all-reduce.4.cloned.1.call-start = ((), (), s32[]{:S(2)}) async-start(), calls=%async_computation.2 | async-start | bytes 1048576 | tf_op jit(solution)/shard_map/psum | solution.py:132
Sparse Core Ops, SparseCore 0:
  283.1 145.1 all-reduce.3
where the time goes:
time: 625 us; the launch traced here: 615 us
  local copies, waits for them, and re-layouts  195 us (31%)
  waiting for transfers between devices  189 us (30%)
  matrix products  62.2 us (10%)
  loops' own time  59.8 us (10%)
  other arithmetic  53 us (8%)
  blocking collectives  27.7 us (4%)
  between operations  15.2 us (2%)
  starting transfers between devices  12.7 us (2%)
    dynamic_update_slice x16, local copies, waits for them, and re-layouts, add_piece(): return lax.dynamic_update_slice(accumulated, current + piece_value, start)  103 us
    all_to_all x1, waiting for transfers between devices, on_device(): lax.all_to_all(returned, 'scan', split_axis=0, concat_axis=0, tiled=True)  96.1 us
    all_to_all x1, waiting for transfers between devices, on_device(): lax.all_to_all(windows, 'scan', split_axis=0, concat_axis=0, tiled=True)  92.4 us
    another operation x1, loops' own time, on_device(): lax.fori_loop(0, scan_count, add_piece, jnp.zeros(extended.shape, jnp.flo...  59.8 us
    gather x48, local copies, waits for them, and re-layouts  44.1 us
    add x16, other arithmetic, add_piece(): return lax.dynamic_update_slice(accumulated, current + piece_value, start)  32.6 us
    dynamic_slice x32, local copies, waits for them, and re-layouts, add_piece(): start = (zero_index, row_offsets[source], col_offsets[source])  20.5 us
    all_gather x1, blocking collectives, on_device(): lax.all_gather(positions, 'scan', axis=2, tiled=True)  19.8 us
  transfers between devices with their start and end apart: 3, of which 2 were waited for; matrix products, arithmetic and copies ran while one was open for 28% of the time, Pallas kernels for 0%

commit v1 on v0

v1 whole, which is shorter than its diff:
```python
import functools
import math

import jax
import jax.numpy as jnp
import numpy as np
from jax import lax
from jax.experimental import pallas as pl
from jax.experimental.pallas import tpu as pltpu
from jax.sharding import PartitionSpec as P

MESH = pl.DeviceIdType.MESH
ANY = pl.BlockSpec(memory_space=pl.ANY)
VMEM = pl.BlockSpec(memory_space=pltpu.VMEM)
ROWS16 = 16


def ring_place(count):
    me = lax.axis_index("scan")
    core = lax.rem(me, 2)
    pair = me // 2
    pos = jnp.where(lax.rem(pair, 2) == 0, pair // 2, count // 2 - 1 - pair // 2)
    return me, core, pos


def pair_at(pos, count):
    pairs = count // 2
    pos = lax.rem(pos + 2 * pairs, pairs)
    return jnp.where(pos < pairs // 2, 2 * pos, 2 * (pairs - 1 - pos) + 1)


def greet(devices):
    barrier = pltpu.get_barrier_semaphore()
    for device in devices:
        pl.semaphore_signal(barrier, inc=1, device_id={"scan": device}, device_id_type=MESH)
    pl.semaphore_wait(barrier, len(devices))


def remote(src, dst, send_sem, recv_sem, device):
    return pltpu.make_async_remote_copy(
        src_ref=src,
        dst_ref=dst,
        send_sem=send_sem,
        recv_sem=recv_sem,
        device_id={"scan": device},
        device_id_type=MESH,
    )


def gather_kernel(count, x_ref, out_ref, zero_ref, zeros, ring_send, ring_recv, pair_send, pair_recv, own_sem, zero_sem):
    me, core, pos = ring_place(count)
    reach = count // 4
    rows = x_ref.shape[1]
    other = me + 1 - 2 * core
    aims = (pair_at(pos + 1, count) * 2 + core, pair_at(pos - 1, count) * 2 + core)
    greet(aims + (other,))

    def slot(distance, which, plane):
        owner = pair_at(pos + distance, count) * 2 + which
        return out_ref.at[plane, pl.ds(pl.multiple_of(owner * rows, rows), rows), :]

    sent = []

    def launch(copy):
        copy.start()
        sent.append(copy)

    def ring_copy(src, way, hop, plane, distance):
        return remote(
            src, slot(distance, core, plane), ring_send.at[way, hop, plane], ring_recv.at[way, hop, plane], aims[way]
        )

    def pair_copy(src, index, plane, distance, which):
        return remote(
            src, slot(distance, which, plane), pair_send.at[index, plane], pair_recv.at[index, plane], other
        )

    for plane in range(2):
        for way in range(2):
            launch(ring_copy(x_ref.at[plane], way, 0, plane, 0))
    for plane in range(2):
        launch(pair_copy(x_ref.at[plane], 0, plane, 0, core))
    own = [pltpu.make_async_copy(x_ref.at[plane], slot(0, core, plane), own_sem.at[plane]) for plane in range(2)]
    for copy in own:
        copy.start()
    zeros[...] = jnp.zeros_like(zeros)
    depth = zeros.shape[1]
    cleared = [
        pltpu.make_async_copy(zeros, zero_ref.at[:, pl.ds(part * depth, depth), :], zero_sem.at[part])
        for part in range(zero_ref.shape[1] // depth)
    ]
    for copy in cleared:
        copy.start()
    for hop in range(reach):
        for plane in range(2):
            for way in range(2):
                if hop == reach - 1 and plane != way:
                    continue
                distance = -(hop + 1) if way == 0 else hop + 1
                here = slot(distance, core, plane)
                ring_copy(here, way, hop, plane, distance).wait_recv()
                if hop < reach - 2 or (hop == reach - 2 and plane == way):
                    launch(ring_copy(here, way, hop + 1, plane, distance))
                index = 1 + 2 * hop + way
                launch(pair_copy(here, index, plane, distance, core))
    for plane in range(2):
        pair_copy(slot(0, 1 - core, plane), 0, plane, 0, 1 - core).wait_recv()
    for hop in range(reach):
        for plane in range(2):
            for way in range(2):
                if hop == reach - 1 and plane != way:
                    continue
                distance = -(hop + 1) if way == 0 else hop + 1
                index = 1 + 2 * hop + way
                pair_copy(slot(distance, 1 - core, plane), index, plane, distance, 1 - core).wait_recv()
    for copy in sent:
        copy.wait_send()
    for copy in own + cleared:
        copy.wait()


def gather_object(tile_low, count):
    planes, rows, columns = tile_low.shape
    whole = jax.ShapeDtypeStruct((planes, count * rows, columns), tile_low.dtype)
    reach = count // 4
    dma = pltpu.SemaphoreType.DMA
    return pl.pallas_call(
        functools.partial(gather_kernel, count),
        out_shape=(whole, whole),
        in_specs=[ANY],
        out_specs=(ANY, ANY),
        scratch_shapes=[
            pltpu.VMEM((planes, 2 * rows, columns), tile_low.dtype),
            dma((2, reach, 2)),
            dma((2, reach, 2)),
            dma((2 * reach + 1, 2)),
            dma((2 * reach + 1, 2)),
            dma((2,)),
            dma((count // 2,)),
        ],
        compiler_params=pltpu.CompilerParams(
            collective_id=0, has_side_effects=True, vmem_limit_bytes=16 * 2**20
        ),
        name="gather_object",
    )(tile_low)


def split(value):
    high = value.astype(jnp.bfloat16)
    return high, (value - high.astype(jnp.float32)).astype(jnp.bfloat16)


def dot(left, right):
    return jnp.dot(left, right, preferred_element_type=jnp.float32)


def product_left(high, low, value):
    first, second = split(value)
    return dot(high[...], first) + (dot(low[...], first) + dot(high[...], second))


def product_right(value, high, low):
    first, second = split(value)
    return dot(first, high[...]) + (dot(first, low[...]) + dot(second, high[...]))


def transform(real_part, imag_part, left, right):
    pixels = real_part.shape[0]
    upright = product_left(*left, jnp.concatenate([real_part, imag_part], axis=0))
    flat = jnp.concatenate([upright[:pixels], upright[pixels:]], axis=1)
    out = product_right(flat, *right)
    return out[:, :pixels], out[:, pixels:]


def pattern_kernel(
    row_ref, col_ref, live_ref, probe_ref, measured_ref, fh_ref, fl_ref, gh_ref, gl_ref, object_ref, blank_ref,
    steps_ref, sum_ref, windows, staged, in_sem, out_sem,
):
    del blank_ref
    slot = pl.program_id(0)
    slots = windows.shape[0]
    pixels = probe_ref.shape[1]
    tall = windows.shape[2]
    stripe = windows.shape[3]

    def aligned(index):
        return pl.multiple_of(row_ref[index] // ROWS16 * ROWS16, ROWS16)

    def fetch(index):
        return pltpu.make_async_copy(
            object_ref.at[:, pl.ds(aligned(index), tall), :], windows.at[index], in_sem.at[index]
        )

    def emit(index):
        return pltpu.make_async_copy(
            staged.at[index], steps_ref.at[:, pl.ds(aligned(index), tall), :], out_sem.at[index]
        )

    @pl.when(slot == 0)
    def _():
        for index in range(slots):
            fetch(index).start()
        sum_ref[...] = jnp.zeros_like(sum_ref)

    fetch(slot).wait()
    row_off = lax.rem(row_ref[slot], ROWS16)
    col = col_ref[slot]
    place = lax.broadcasted_iota(jnp.int32, (stripe, pixels), 0) - lax.broadcasted_iota(
        jnp.int32, (stripe, pixels), 1
    )
    pick = jnp.where(place == col, 1.0, 0.0).astype(jnp.bfloat16)

    def cut(plane):
        moved = dot(windows[slot, plane], pick)
        return pltpu.roll(moved, lax.rem(tall - row_off, tall), 0)[:pixels]

    object_real = cut(0)
    object_imag = cut(1)
    probe_real = probe_ref[0]
    probe_imag = probe_ref[1]
    forward, backward = (fh_ref, fl_ref), (gh_ref, gl_ref)
    far_real, far_imag = transform(
        probe_real * object_real - probe_imag * object_imag,
        probe_real * object_imag + probe_imag * object_real,
        forward,
        backward,
    )
    misfit = far_real * far_real + far_imag * far_imag - measured_ref[0]
    back_real, back_imag = transform(misfit * far_real, misfit * far_imag, backward, forward)
    living = jnp.where(slot < live_ref[0], 1.0, 0.0).astype(jnp.float32)
    back_real = back_real * living
    back_imag = back_imag * living
    sum_ref[0] += object_real * back_real + object_imag * back_imag
    sum_ref[1] += object_real * back_imag - object_imag * back_real

    def put(plane, value):
        low = value.astype(jnp.bfloat16).astype(jnp.float32)
        padded = jnp.concatenate([low, jnp.zeros((tall - pixels, pixels), jnp.float32)], axis=0)
        moved = pltpu.roll(padded, row_off, 0).astype(jnp.bfloat16)
        spread = lax.dot_general(moved, pick, (((1,), (1,)), ((), ())), preferred_element_type=jnp.float32)
        staged[slot, plane] = spread.astype(jnp.bfloat16)

    put(0, probe_real * back_real + probe_imag * back_imag)
    put(1, probe_real * back_imag - probe_imag * back_real)
    emit(slot).start()

    @pl.when(slot == slots - 1)
    def _():
        for index in range(slots):
            emit(index).wait()


def dft_tables(pixels):
    counter = np.arange(pixels)
    angle = (counter[:, None] * counter[None, :] % pixels) * (2.0 * math.pi / pixels)
    cosine = np.cos(angle) / math.sqrt(pixels)
    sine = np.sin(angle) / math.sqrt(pixels)
    tables = []
    for table in (np.block([[cosine, sine], [-sine, cosine]]), np.block([[cosine, -sine], [sine, cosine]])):
        table = table.astype(np.float32)
        high = table.astype(jnp.bfloat16)
        tables += [high, (table - high.astype(np.float32)).astype(jnp.bfloat16)]
    return tables


def pattern_steps(whole, blank, probe_field, measured, rows, cols, live):
    slots, pixels, _ = measured.shape
    stripe = whole.shape[2]
    tall = pixels + ROWS16
    smem = pl.BlockSpec(memory_space=pltpu.SMEM)
    tables = dft_tables(pixels)
    plane = pl.BlockSpec((2, pixels, pixels), lambda slot: (0, 0, 0))
    table = pl.BlockSpec((2 * pixels, 2 * pixels), lambda slot: (0, 0))
    return pl.pallas_call(
        pattern_kernel,
        grid=(slots,),
        out_shape=(
            jax.ShapeDtypeStruct(blank.shape, blank.dtype),
            jax.ShapeDtypeStruct(probe_field.shape, jnp.float32),
        ),
        in_specs=[
            smem, smem, smem, plane, pl.BlockSpec((1, pixels, pixels), lambda slot: (slot, 0, 0)),
            table, table, table, table, ANY, ANY,
        ],
        out_specs=(ANY, plane),
        scratch_shapes=[
            pltpu.VMEM((slots, 2, tall, stripe), jnp.bfloat16),
            pltpu.VMEM((slots, 2, tall, stripe), jnp.bfloat16),
            pltpu.SemaphoreType.DMA((slots,)),
            pltpu.SemaphoreType.DMA((slots,)),
        ],
        input_output_aliases={10: 0},
        compiler_params=pltpu.CompilerParams(vmem_limit_bytes=40 * 2**20),
        name="pattern_steps",
    )(rows, cols, live, probe_field, measured, *tables, whole, blank)


def reduce_kernel(
    count, x_ref, probe_ref, out_ref, probe_out_ref, own, sib, inbox, pown, psib, pinbox, pfinal,
    own_sem, sib_send, sib_recv, ring_send, ring_recv,
    pown_sem, psib_send, psib_recv, pring_send, pring_recv, all_send, all_recv, mate_send, mate_recv, last_sem,
):
    me, core, pos = ring_place(count)
    pairs = count // 2
    reach = pairs // 2
    rows = own.shape[2]
    other = me + 1 - 2 * core
    aims = (pair_at(pos + 1, count) * 2 + core, pair_at(pos - 1, count) * 2 + core)
    greet(aims + (other,))
    sent = []

    def launch(copy):
        copy.start()
        sent.append(copy)

    def band(rel, which, plane):
        owner = pair_at(pos + rel, count) * 2 + which
        return x_ref.at[plane, pl.ds(pl.multiple_of(owner * rows, rows), rows), :]

    def own_copy(rel, plane):
        return pltpu.make_async_copy(band(rel, core, plane), own.at[rel, plane], own_sem.at[rel, plane])

    def sib_copy(rel, plane):
        return remote(
            band(rel, 1 - core, plane), sib.at[rel, plane], sib_send.at[rel, plane], sib_recv.at[rel, plane], other
        )

    def pown_copy(rel):
        return pltpu.make_async_copy(
            probe_ref.at[:, pair_at(pos + rel, count), core], pown.at[rel], pown_sem.at[rel]
        )

    def psib_copy(rel):
        return remote(
            probe_ref.at[:, pair_at(pos + rel, count), 1 - core], psib.at[rel], psib_send.at[rel], psib_recv.at[rel],
            other,
        )

    order = [reach]
    for k in range(reach - 1, 0, -1):
        order += [k, pairs - k]
    order += [0]
    for rel in order[:1]:
        pown_copy(rel).start()
        launch(psib_copy(rel))
        for plane in range(2):
            own_copy(rel, plane).start()
            launch(sib_copy(rel, plane))
    for rel in order[1:]:
        pown_copy(rel).start()
        launch(psib_copy(rel))
    for rel in order[1:]:
        for plane in range(2):
            own_copy(rel, plane).start()
            launch(sib_copy(rel, plane))

    def ring_copy(way, rel, k, plane):
        return remote(
            own.at[rel, plane], inbox.at[way, k - 1, plane], ring_send.at[way, k - 1, plane],
            ring_recv.at[way, k - 1, plane], aims[way],
        )

    def add_rows(target, terms):
        block = 64

        def body(index, carry):
            at = pl.ds(pl.multiple_of(index * block, block), block)
            total = terms[0][at, :].astype(jnp.float32)
            for term in terms[1:]:
                total = total + term[at, :].astype(jnp.float32)
            target[at, :] = total.astype(target.dtype)
            return carry

        lax.fori_loop(0, rows // block, body, 0)

    def main_hop(way, k, plane):
        rel = k if way == 0 else pairs - k
        own_copy(rel, plane).wait()
        sib_copy(rel, plane).wait_recv()
        terms = [own.at[rel, plane], sib.at[rel, plane]]
        if k < reach and not (k == reach - 1 and plane != way):
            ring_copy(way, rel, k + 1, plane).wait_recv()
            terms.append(inbox.at[way, k, plane])
        add_rows(own.at[rel, plane], terms)
        launch(ring_copy(way, rel, k, plane))

    def pring_copy(way, rel, k):
        if k == reach:
            return remote(
                pown.at[rel, way], pinbox.at[way, k - 1, way], pring_send.at[way, k - 1], pring_recv.at[way, k - 1],
                aims[way],
            )
        return remote(
            pown.at[rel], pinbox.at[way, k - 1], pring_send.at[way, k - 1], pring_recv.at[way, k - 1], aims[way]
        )

    def probe_hop(k):
        if k == reach:
            pown_copy(reach).wait()
            psib_copy(reach).wait_recv()
            pown[reach] = pown[reach] + psib[reach]
            for way in range(2):
                launch(pring_copy(way, reach, k))
            return
        for way in range(2):
            rel = k if way == 0 else pairs - k
            pown_copy(rel).wait()
            psib_copy(rel).wait_recv()
            pring_copy(way, rel, k + 1).wait_recv()
            pown[rel] = pown[rel] + psib[rel]
            if k == reach - 1:
                pown[rel, way] = pown[rel, way] + pinbox[way, k, way]
            else:
                pown[rel] = pown[rel] + pinbox[way, k]
            launch(pring_copy(way, rel, k))

    def result(distance, which):
        return probe_out_ref.at[:, pair_at(pos + distance, count), which]

    def all_copy(src, way, hop, distance):
        if hop == reach - 1:
            place = probe_out_ref.at[way, pair_at(pos + distance, count), core]
        else:
            place = result(distance, core)
        return remote(src, place, all_send.at[way, hop], all_recv.at[way, hop], aims[way])

    def mate_copy(src, index, distance, which, plane=None):
        place = result(distance, which)
        if plane is not None:
            place = probe_out_ref.at[plane, pair_at(pos + distance, count), which]
        return remote(src, place, mate_send.at[index], mate_recv.at[index], other)

    last = pltpu.make_async_copy(pfinal, result(0, core), last_sem)

    def probe_finish():
        pown_copy(0).wait()
        psib_copy(0).wait_recv()
        total = pown[0] + psib[0]
        for way in range(2):
            pring_copy(way, 0, 1).wait_recv()
            total = total + pinbox[way, 0]
        pfinal[...] = total
        for way in range(2):
            launch(all_copy(pfinal, way, 0, 0))
        launch(mate_copy(pfinal, 0, 0, core))
        last.start()

    def probe_spread(hop):
        for way in range(2):
            distance = -(hop + 1) if way == 0 else hop + 1
            end = hop == reach - 1
            half = probe_out_ref.at[way, pair_at(pos + distance, count), core]
            here = half if end else result(distance, core)
            all_copy(here, way, hop, distance).wait_recv()
            if not end:
                launch(all_copy(half if hop == reach - 2 else here, way, hop + 1, distance))
            launch(mate_copy(here, 1 + 2 * hop + way, distance, core, way if end else None))

    stages = [functools.partial(probe_hop, k) for k in range(reach, 0, -1)]
    stages += [probe_finish]
    stages += [functools.partial(probe_spread, hop) for hop in range(reach)]
    hops = [[(0, reach, 0), (1, reach, 1)]]
    for k in range(reach - 1, 0, -1):
        for plane in range(2):
            hops.append([(0, k, 1 - plane), (1, k, plane)])
    while stages or hops:
        if stages:
            stages.pop(0)()
        if hops:
            for hop in hops.pop(0):
                main_hop(*hop)

    for plane in range(2):
        own_copy(0, plane).wait()
        sib_copy(0, plane).wait_recv()
        for way in range(2):
            ring_copy(way, 0, 1, plane).wait_recv()
        add_rows(
            out_ref.at[plane], [own.at[0, plane], sib.at[0, plane], inbox.at[0, 0, plane], inbox.at[1, 0, plane]]
        )
    mate_copy(result(0, 1 - core), 0, 0, 1 - core).wait_recv()
    for hop in range(reach):
        for way in range(2):
            distance = -(hop + 1) if way == 0 else hop + 1
            end = hop == reach - 1
            there = probe_out_ref.at[way, pair_at(pos + distance, count), 1 - core] if end else result(distance, 1 - core)
            mate_copy(there, 1 + 2 * hop + way, distance, 1 - core, way if end else None).wait_recv()
    last.wait()
    for copy in sent:
        copy.wait_send()


def reduce_steps(steps, probe_part, count):
    planes, long_rows, columns = steps.shape
    rows = long_rows // count
    pixels = probe_part.shape[1]
    pairs = count // 2
    reach = pairs // 2
    share = pixels // count
    dma = pltpu.SemaphoreType.DMA
    grad, total = pl.pallas_call(
        functools.partial(reduce_kernel, count),
        out_shape=(
            jax.ShapeDtypeStruct((planes, rows, columns), jnp.float32),
            jax.ShapeDtypeStruct((2, pairs, 2, share, pixels), jnp.float32),
        ),
        in_specs=[ANY, ANY],
        out_specs=(VMEM, ANY),
        scratch_shapes=[
            pltpu.VMEM((pairs, 2, rows, columns), jnp.bfloat16),
            pltpu.VMEM((pairs, 2, rows, columns), jnp.bfloat16),
            pltpu.VMEM((2, reach, 2, rows, columns), jnp.bfloat16),
            pltpu.VMEM((pairs, 2, share, pixels), jnp.float32),
            pltpu.VMEM((pairs, 2, share, pixels), jnp.float32),
            pltpu.VMEM((2, reach, 2, share, pixels), jnp.float32),
            pltpu.VMEM((2, share, pixels), jnp.float32),
            dma((pairs, 2)),
            dma((pairs, 2)),
            dma((pairs, 2)),
            dma((2, reach, 2)),
            dma((2, reach, 2)),
            dma((pairs,)),
            dma((pairs,)),
            dma((pairs,)),
            dma((2, reach)),
            dma((2, reach)),
            dma((2, reach)),
            dma((2, reach)),
            dma((2 * reach + 1,)),
            dma((2 * reach + 1,)),
            dma,
        ],
        compiler_params=pltpu.CompilerParams(
            collective_id=1, has_side_effects=True, vmem_limit_bytes=40 * 2**20
        ),
        name="reduce_steps",
    )(steps, probe_part.reshape(2, pairs, 2, share, pixels))
    return grad, total.reshape(2, pixels, pixels)


def on_device(object_field, probe_field, intensities, positions, live_counts):
    pixels = probe_field.shape[1]
    stripe = object_field.shape[2]
    slots = positions.shape[2]
    count = lax.axis_size("scan")
    whole, blank = gather_object(object_field.astype(jnp.bfloat16), count)
    places = positions.reshape(slots, 2)
    steps, probe_part = pattern_steps(
        whole,
        blank,
        probe_field,
        intensities.reshape(slots, pixels, pixels),
        places[:, 0],
        places[:, 1] - lax.axis_index("obj") * stripe,
        live_counts.reshape(1),
    )
    object_grad, probe_grad = reduce_steps(steps, probe_part, count)
    if lax.axis_size("sub") > 1:
        object_grad = lax.psum(object_grad, "sub")
    if lax.axis_size("obj") * lax.axis_size("sub") > 1:
        probe_grad = lax.psum(probe_grad, ("obj", "sub"))
    return (object_grad, probe_grad)


def solution(mesh):
    placed = (
        P(None, ("groups", "scan"), "obj"),
        P("groups", None, None),
        P(("groups", "obj"), "sub", "scan", None, None),
        P(("groups", "obj"), "sub", "scan", None),
        P(("groups", "obj"), "sub", "scan"),
    )
    return jax.shard_map(
        on_device,
        mesh=mesh,
        in_specs=placed,
        out_specs=(P(None, ("groups", "scan"), "obj"), P("groups", None, None)),
        check_vma=False,
    )
```

time: 625 us -> 146 us (0.23); the launches traced: 615 us -> 143 us
  waiting for transfers between devices: 189 us -> 0 us
  local copies, waits for them, and re-layouts: 195 us -> 12.4 us
  Pallas kernels: 0 us -> 128 us
  matrix products: 62.2 us -> 0 us
  loops' own time: 59.8 us -> 0 us
  other arithmetic: 53 us -> 1.29 us
  blocking collectives: 27.7 us -> 0 us
  between operations: 15.2 us -> 1.32 us
  starting transfers between devices: 12.7 us -> 0 us
    all_to_all x2 -> x0, waiting for transfers between devices: 189 us -> none  [the longest x1 96.1 us: on_device(): lax.all_to_all(returned, 'scan', split_axis=0, concat_axis=0, tiled=True)]
    pallas_call x0 -> x3, Pallas kernels: none -> 128 us  [the longest x1 51.7 us: reduce_steps(): pl.pallas_call(functools.partial(reduce_kernel, count), out_shape=(jax.Sh...]
    dynamic_update_slice x16 -> x0, local copies, waits for them, and re-layouts: 103 us -> none  [add_piece(): return lax.dynamic_update_slice(accumulated, current + piece_value, start)]
    dot_general x18 -> x0, matrix products: 62.2 us -> none  [the longest x2 7.73 us: transform(): jnp.einsum('pkn,nm->pkm', left_real, cosine_table, precision=highest)]
    another operation x2 -> x0, loops' own time: 59.8 us -> none  [the longest x1 59.8 us: on_device(): lax.fori_loop(0, scan_count, add_piece, jnp.zeros(extended.shape, jnp.flo...]
    gather x48 -> x0, local copies, waits for them, and re-layouts: 44.1 us -> none
    add x17 -> x0, other arithmetic: 32.6 us -> none  [the longest x16 32.6 us: add_piece(): return lax.dynamic_update_slice(accumulated, current + piece_value, start)]
    dynamic_slice x48 -> x0, local copies, waits for them, and re-layouts: 30.8 us -> none  [the longest x32 20.5 us: add_piece(): start = (zero_index, row_offsets[source], col_offsets[source])]
  transfers between devices with their start and end apart: 3 -> 0, of which waited for: 2 -> 0; matrix products, arithmetic and copies ran while one was open for 28% -> 0% of each run, Pallas kernels for 0% -> 0%
where the time goes in v1:
time: 146 us; the launch traced here: 143 us
  Pallas kernels  128 us (88%)
  local copies, waits for them, and re-layouts  12.4 us (8%)
    pallas_call x1, Pallas kernels, reduce_steps(): pl.pallas_call(functools.partial(reduce_kernel, count), out_shape=(jax.Sh...  51.7 us
    pallas_call x1, Pallas kernels, gather_object(): pl.pallas_call(functools.partial(gather_kernel, count), out_shape=(whole,...  45.8 us
    pallas_call x1, Pallas kernels, pattern_steps(): pl.pallas_call(pattern_kernel, grid=(slots,), out_shape=(jax.ShapeDtypeSt...  30.8 us
    unnamed x16, local copies, waits for them, and re-layouts  11.6 us

profile of v1, /device:TPU:15, one launch (start us, length us, event | category | flops | bytes accessed | tf_op | source)
XLA Modules:
  0.0 143.2 jit_solution(4017695248059634595)
XLA Ops:
  1.3 0.8 slice_bitcast_fusion
  2.0 1.3 convert_element_type.3.x_ref
  3.3 45.8 %gather_object.1 = (bf16[2,4096,512]{2,1,0:T(8,128)(2,1)S(1)}, bf16[2,4096,512]{2,1,0:T(8,128)(2,1)S(1)}) custom-call(bf16[2,256,512]{2,1,0:T(8,128)(2,1)S(1)} %convert_element_type.3.x_ref), custom_call_target="tpu_custom_call" | custom-call | tf_op jit(solution)/shard_map/gather_object/pallas_call | solution.py:127
  49.1 0.0 copy-start
  49.1 3.2 %copy-done = bf16[2,4096,512]{2,1,0:T(8,128)(2,1)} copy-done((bf16[2,4096,512]{2,1,0:T(8,128)(2,1)}, bf16[2,4096,512]{2,1,0:T(8,128)(2,1)S(1)}, u32[]{:S(2)}) %copy-start) | copy-done | bytes 8388632
  52.3 0.0 copy-start.1
  52.3 1.4 copy-done.1
  53.7 0.0 copy-start.2
  53.7 1.0 copy-done.2
  54.8 0.0 copy-start.3
  54.8 1.0 copy-done.3
  55.8 0.0 copy-start.4
  55.8 1.0 copy-done.4
  56.9 0.0 copy-start.5
  56.9 1.0 copy-done.5
  57.9 0.0 copy-start.6
  57.9 1.0 copy-done.6
  58.9 30.8 %pattern_steps.1 = (bf16[2,4096,512]{2,1,0:T(8,128)(2,1)S(1)}, f32[2,256,256]{2,1,0:T(8,128)S(1)}) custom-call(s32[6]{0:T(128)S(1)} %get-tuple-element.15.row_ref, s32[6]{0:T(128)S(1)} %get-tuple-element.14.col_ref, s32[1]{0:T(128)} %bitcast.9.live_ref, f32[2,256,256]{2,1,0:T(8,128)S(1)} %copy-done.2, ...), custom_call_target="tpu_custom_call", output_to_operand_aliasing={{0}: (10, {})} | custom-call | tf_op jit(solution)/shard_map/pattern_steps/pallas_call | solution.py:274
  89.7 51.7 %reduce_steps.1 = (f32[2,256,512]{2,1,0:T(8,128)S(1)}, f32[2,8,2,16,256]{4,3,2,1,0:T(8,128)S(1)}) custom-call(bf16[2,4096,512]{2,1,0:T(8,128)(2,1)S(1)} %get-tuple-element.10.x_ref, f32[2,8,2,16,256]{4,3,2,1,0:T(8,128)S(1)} %bitcast.11), custom_call_target="tpu_custom_call" | custom-call | tf_op jit(solution)/shard_map/reduce_steps/pallas_call | solution.py:501
  141.5 1.0 copy.16
  142.4 0.8 copy.17
Async XLA Ops:
  49.1 3.2 %copy-start = (bf16[2,4096,512]{2,1,0:T(8,128)(2,1)}, bf16[2,4096,512]{2,1,0:T(8,128)(2,1)S(1)}, u32[]{:S(2)}) copy-start(bf16[2,4096,512]{2,1,0:T(8,128)(2,1)S(1)} %get-tuple-element.8.object_ref) | copy-start | bytes 25165828
  52.3 1.4 copy-start.1
  53.7 1.0 copy-start.2
  54.8 1.0 copy-start.3
  55.8 1.0 copy-start.4
  56.9 1.0 copy-start.5
  57.9 1.0 copy-start.6

commit v2 on v1

--- a/solution.py
+++ b/solution.py
@@ -150,35 +150,83 @@
     return high, (value - high.astype(jnp.float32)).astype(jnp.bfloat16)
 
 
-def dot(left, right):
-    return jnp.dot(left, right, preferred_element_type=jnp.float32)
-
-
-def product_left(high, low, value):
+def product_left(table, value):
     first, second = split(value)
-    return dot(high[...], first) + (dot(low[...], first) + dot(high[...], second))
-
-
-def product_right(value, high, low):
+    terms = jnp.concatenate([first, first, second], axis=0)
+    return jnp.dot(table[...], terms, preferred_element_type=jnp.float32)
+
+
+def product_right(value, table):
     first, second = split(value)
-    return dot(first, high[...]) + (dot(first, low[...]) + dot(second, high[...]))
-
-
-def transform(real_part, imag_part, left, right):
-    pixels = real_part.shape[0]
-    upright = product_left(*left, jnp.concatenate([real_part, imag_part], axis=0))
-    flat = jnp.concatenate([upright[:pixels], upright[pixels:]], axis=1)
-    out = product_right(flat, *right)
-    return out[:, :pixels], out[:, pixels:]
+    terms = jnp.concatenate([first, first, second], axis=1)
+    return jnp.dot(terms, table[...], preferred_element_type=jnp.float32)
+
+
+def halves(value, axis):
+    middle = value.shape[axis] // 2
+    if axis == 0:
+        return value[:middle], value[middle:]
+    return value[:, :middle], value[:, middle:]
+
+
+def multiply(even, odd, tables, axis):
+    found = []
+    for table, parts in zip(tables, (even, odd)):
+        stacked = jnp.concatenate([jnp.concatenate(part, axis=axis) for part in parts], axis=1 - axis)
+        out = product_left(table, stacked) if axis == 0 else product_right(stacked, table)
+        size = out.shape[1 - axis] // len(parts)
+        planes = [
+            out[:, index * size : (index + 1) * size] if axis == 0 else out[index * size : (index + 1) * size]
+            for index in range(len(parts))
+        ]
+        found.append([halves(plane, axis) for plane in planes])
+    return found
+
+
+def ahead(waves, tables, axis):
+    even, odd = [], []
+    for wave in waves:
+        split_parts = [halves(part, axis) for part in wave]
+        even.append([first + second for first, second in split_parts])
+        odd.append([first - second for first, second in split_parts])
+    found = multiply(even, odd, tables, axis)
+    return [
+        tuple(jnp.concatenate([one, two], axis=axis) for one, two in zip(low, high)) for low, high in zip(*found)
+    ]
+
+
+def behind(waves, tables, axis):
+    even = [[halves(part, axis)[0] for part in wave] for wave in waves]
+    odd = [[halves(part, axis)[1] for part in wave] for wave in waves]
+    found = multiply(even, odd, tables, axis)
+    return [
+        tuple(jnp.concatenate([one + two, one - two], axis=axis) for one, two in zip(low, high))
+        for low, high in zip(*found)
+    ]
+
+
+def reorder(value, down, across):
+    size = value.shape[0]
+    first, second = split(value)
+    both = jnp.dot(jnp.concatenate([first, second], axis=0), across, preferred_element_type=jnp.float32)
+    both = both.astype(jnp.bfloat16)
+    both = jnp.concatenate([both[:size], both[size:]], axis=1)
+    both = jnp.dot(down, both, preferred_element_type=jnp.float32)
+    return both[:, :size] + both[:, size:]
+
+
+GROUP = 3
 
 
 def pattern_kernel(
-    row_ref, col_ref, live_ref, probe_ref, measured_ref, fh_ref, fl_ref, gh_ref, gl_ref, object_ref, blank_ref,
-    steps_ref, sum_ref, windows, staged, in_sem, out_sem,
+    row_ref, col_ref, live_ref, probe_ref, measured_ref, down_ref, across_ref, *rest,
 ):
+    tables, rest = rest[:8], rest[8:]
+    (object_ref, blank_ref, steps_ref, sum_ref, windows, staged, in_sem, out_sem) = rest
     del blank_ref
-    slot = pl.program_id(0)
+    turn = pl.program_id(0)
     slots = windows.shape[0]
+    group = measured_ref.shape[0]
     pixels = probe_ref.shape[1]
     tall = windows.shape[2]
     stripe = windows.shape[3]
@@ -196,70 +244,100 @@
             staged.at[index], steps_ref.at[:, pl.ds(aligned(index), tall), :], out_sem.at[index]
         )
 
-    @pl.when(slot == 0)
+    @pl.when(turn == 0)
     def _():
         for index in range(slots):
             fetch(index).start()
         sum_ref[...] = jnp.zeros_like(sum_ref)
 
-    fetch(slot).wait()
-    row_off = lax.rem(row_ref[slot], ROWS16)
-    col = col_ref[slot]
-    place = lax.broadcasted_iota(jnp.int32, (stripe, pixels), 0) - lax.broadcasted_iota(
+    for member in range(group):
+        fetch(turn * group + member).wait()
+    apart = lax.broadcasted_iota(jnp.int32, (stripe, pixels), 0) - lax.broadcasted_iota(
         jnp.int32, (stripe, pixels), 1
     )
-    pick = jnp.where(place == col, 1.0, 0.0).astype(jnp.bfloat16)
-
-    def cut(plane):
-        moved = dot(windows[slot, plane], pick)
-        return pltpu.roll(moved, lax.rem(tall - row_off, tall), 0)[:pixels]
-
-    object_real = cut(0)
-    object_imag = cut(1)
+    picks, patches, waves = [], [], []
     probe_real = probe_ref[0]
     probe_imag = probe_ref[1]
-    forward, backward = (fh_ref, fl_ref), (gh_ref, gl_ref)
-    far_real, far_imag = transform(
-        probe_real * object_real - probe_imag * object_imag,
-        probe_real * object_imag + probe_imag * object_real,
-        forward,
-        backward,
-    )
-    misfit = far_real * far_real + far_imag * far_imag - measured_ref[0]
-    back_real, back_imag = transform(misfit * far_real, misfit * far_imag, backward, forward)
-    living = jnp.where(slot < live_ref[0], 1.0, 0.0).astype(jnp.float32)
-    back_real = back_real * living
-    back_imag = back_imag * living
-    sum_ref[0] += object_real * back_real + object_imag * back_imag
-    sum_ref[1] += object_real * back_imag - object_imag * back_real
-
-    def put(plane, value):
-        low = value.astype(jnp.bfloat16).astype(jnp.float32)
-        padded = jnp.concatenate([low, jnp.zeros((tall - pixels, pixels), jnp.float32)], axis=0)
-        moved = pltpu.roll(padded, row_off, 0).astype(jnp.bfloat16)
-        spread = lax.dot_general(moved, pick, (((1,), (1,)), ((), ())), preferred_element_type=jnp.float32)
-        staged[slot, plane] = spread.astype(jnp.bfloat16)
-
-    put(0, probe_real * back_real + probe_imag * back_imag)
-    put(1, probe_real * back_imag - probe_imag * back_real)
-    emit(slot).start()
-
-    @pl.when(slot == slots - 1)
+    for member in range(group):
+        slot = turn * group + member
+        pick = jnp.where(apart == col_ref[slot], 1.0, 0.0).astype(jnp.bfloat16)
+        both = jnp.concatenate([windows[slot, 0], windows[slot, 1]], axis=0)
+        moved = jnp.dot(both, pick, preferred_element_type=jnp.float32)
+        shift = lax.rem(tall - lax.rem(row_ref[slot], ROWS16), tall)
+        object_real = pltpu.roll(moved[:tall], shift, 0)[:pixels]
+        object_imag = pltpu.roll(moved[tall:], shift, 0)[:pixels]
+        picks.append(pick)
+        patches.append((object_real, object_imag))
+        waves.append(
+            (
+                probe_real * object_real - probe_imag * object_imag,
+                probe_real * object_imag + probe_imag * object_real,
+            )
+        )
+    far = ahead(ahead(waves, tables[0:2], 0), tables[2:4], 1)
+    weighted = []
+    for member in range(group):
+        far_real, far_imag = far[member]
+        misfit = far_real * far_real + far_imag * far_imag - reorder(
+            measured_ref[member], down_ref[...], across_ref[...]
+        )
+        weighted.append((misfit * far_real, misfit * far_imag))
+    back = behind(behind(weighted, tables[4:6], 0), tables[6:8], 1)
+    total_real, total_imag = sum_ref[0], sum_ref[1]
+    for member in range(group):
+        slot = turn * group + member
+        living = jnp.where(slot < live_ref[0], 1.0, 0.0).astype(jnp.float32)
+        back_real, back_imag = back[member][0] * living, back[member][1] * living
+        object_real, object_imag = patches[member]
+        total_real += object_real * back_real + object_imag * back_imag
+        total_imag += object_real * back_imag - object_imag * back_real
+        row_off = lax.rem(row_ref[slot], ROWS16)
+
+        def shifted(value):
+            low = value.astype(jnp.bfloat16).astype(jnp.float32)
+            padded = jnp.concatenate([low, jnp.zeros((tall - pixels, pixels), jnp.float32)], axis=0)
+            return pltpu.roll(padded, row_off, 0).astype(jnp.bfloat16)
+
+        both = jnp.concatenate(
+            [
+                shifted(probe_real * back_real + probe_imag * back_imag),
+                shifted(probe_real * back_imag - probe_imag * back_real),
+            ],
+            axis=0,
+        )
+        spread = lax.dot_general(both, picks[member], (((1,), (1,)), ((), ())), preferred_element_type=jnp.float32)
+        spread = spread.astype(jnp.bfloat16)
+        staged[slot, 0] = spread[:tall]
+        staged[slot, 1] = spread[tall:]
+        emit(slot).start()
+    sum_ref[0] = total_real
+    sum_ref[1] = total_imag
+
+    @pl.when(turn == slots // group - 1)
     def _():
         for index in range(slots):
             emit(index).wait()
 
 
 def dft_tables(pixels):
-    counter = np.arange(pixels)
-    angle = (counter[:, None] * counter[None, :] % pixels) * (2.0 * math.pi / pixels)
-    cosine = np.cos(angle) / math.sqrt(pixels)
-    sine = np.sin(angle) / math.sqrt(pixels)
-    tables = []
-    for table in (np.block([[cosine, sine], [-sine, cosine]]), np.block([[cosine, -sine], [sine, cosine]])):
-        table = table.astype(np.float32)
-        high = table.astype(jnp.bfloat16)
-        tables += [high, (table - high.astype(np.float32)).astype(jnp.bfloat16)]
+    half = pixels // 2
+    order = np.concatenate([np.arange(0, pixels, 2), np.arange(1, pixels, 2)])
+    down = np.eye(pixels, dtype=np.float32)[order]
+    tables = [down.astype(jnp.bfloat16), np.ascontiguousarray(down.T).astype(jnp.bfloat16)]
+    point = np.arange(half)
+    kinds = []
+    for odd in range(2):
+        turns = (2 * point[:, None] + odd) * point[None, :] % pixels
+        kinds.append(np.exp(-2j * math.pi * turns / pixels) / math.sqrt(pixels))
+    for place in (lambda kind: kind, lambda kind: kind.T, lambda kind: kind.conj().T, lambda kind: kind.conj()):
+        axis = (len(tables) // 2 + 1) % 2
+        for kind in kinds:
+            kind = place(kind)
+            sign = 1 if axis else -1
+            table = np.block([[kind.real, sign * kind.imag], [-sign * kind.imag, kind.real]]).astype(np.float32)
+            high = table.astype(jnp.bfloat16)
+            low = (table - high.astype(np.float32)).astype(jnp.bfloat16)
+            tables.append(np.concatenate([high, low, high], axis=1 - axis))
     return tables
 
 
@@ -267,20 +345,20 @@
     slots, pixels, _ = measured.shape
     stripe = whole.shape[2]
     tall = pixels + ROWS16
+    group = GROUP if slots % GROUP == 0 else 1
     smem = pl.BlockSpec(memory_space=pltpu.SMEM)
     tables = dft_tables(pixels)
-    plane = pl.BlockSpec((2, pixels, pixels), lambda slot: (0, 0, 0))
-    table = pl.BlockSpec((2 * pixels, 2 * pixels), lambda slot: (0, 0))
+    plane = pl.BlockSpec((2, pixels, pixels), lambda turn: (0, 0, 0))
     return pl.pallas_call(
         pattern_kernel,
-        grid=(slots,),
+        grid=(slots // group,),
         out_shape=(
             jax.ShapeDtypeStruct(blank.shape, blank.dtype),
             jax.ShapeDtypeStruct(probe_field.shape, jnp.float32),
         ),
         in_specs=[
-            smem, smem, smem, plane, pl.BlockSpec((1, pixels, pixels), lambda slot: (slot, 0, 0)),
-            table, table, table, table, ANY, ANY,
+            smem, smem, smem, plane, pl.BlockSpec((group, pixels, pixels), lambda turn: (turn, 0, 0)),
+            *[pl.BlockSpec(table.shape, lambda turn: (0, 0)) for table in tables], ANY, ANY,
         ],
         out_specs=(ANY, plane),
         scratch_shapes=[
@@ -289,8 +367,8 @@
             pltpu.SemaphoreType.DMA((slots,)),
             pltpu.SemaphoreType.DMA((slots,)),
         ],
-        input_output_aliases={10: 0},
-        compiler_params=pltpu.CompilerParams(vmem_limit_bytes=40 * 2**20),
+        input_output_aliases={6 + len(tables): 0},
+        compiler_params=pltpu.CompilerParams(vmem_limit_bytes=60 * 2**20),
         name="pattern_steps",
     )(rows, cols, live, probe_field, measured, *tables, whole, blank)
 

time: 146 us -> 134 us (0.918)
  Pallas kernels: 128 us -> 115 us
  local copies, waits for them, and re-layouts: 12.4 us -> 14 us
    pallas_call x1, Pallas kernels: 30.8 us -> 17.3 us  [pattern_steps(): pl.pallas_call(pattern_kernel, grid=(slots // group,), out_shape=(jax.Sha...]
    unnamed x16 -> x10, local copies, waits for them, and re-layouts: 11.6 us -> 12.6 us
where the time goes in v2:
time: 134 us; the launch traced here: 131 us
  Pallas kernels  115 us (86%)
  local copies, waits for them, and re-layouts  14 us (10%)
    pallas_call x1, Pallas kernels, reduce_steps(): pl.pallas_call(functools.partial(reduce_kernel, count), out_shape=(jax.Sh...  51.7 us
    pallas_call x1, Pallas kernels, gather_object(): pl.pallas_call(functools.partial(gather_kernel, count), out_shape=(whole,...  45.8 us
    pallas_call x1, Pallas kernels, pattern_steps(): pl.pallas_call(pattern_kernel, grid=(slots // group,), out_shape=(jax.Sha...  17.3 us
    unnamed x10, local copies, waits for them, and re-layouts  12.6 us

profile of v2, /device:TPU:15, one launch (start us, length us, event | category | flops | bytes accessed | tf_op | source)
XLA Modules:
  0.0 131.3 jit_solution(359718797265810606)
XLA Ops:
  1.3 1.3 %slice_bitcast_fusion = (s32[6]{0:T(128)}, s32[6]{0:T(128)}) fusion(s32[6,2]{0,1:T(2,128)} %bitcast.13), kind=kLoop, calls=%fused_computation | loop fusion | bytes 96 | tf_op jit(solution)/shard_map/squeeze | solution.py:632
  2.6 1.3 convert_element_type.3.x_ref
  3.9 45.8 %gather_object.1 = (bf16[2,4096,512]{2,1,0:T(8,128)(2,1)S(1)}, bf16[2,4096,512]{2,1,0:T(8,128)(2,1)S(1)}) custom-call(bf16[2,256,512]{2,1,0:T(8,128)(2,1)S(1)} %convert_element_type.3.x_ref), custom_call_target="tpu_custom_call" | custom-call | tf_op jit(solution)/shard_map/gather_object/pallas_call | solution.py:127
  49.7 0.0 copy-start
  49.7 3.2 %copy-done = bf16[2,4096,512]{2,1,0:T(8,128)(2,1)} copy-done((bf16[2,4096,512]{2,1,0:T(8,128)(2,1)}, bf16[2,4096,512]{2,1,0:T(8,128)(2,1)S(1)}, u32[]{:S(2)}) %copy-start) | copy-done | bytes 8388632
  52.9 0.0 copy-start.2
  52.9 3.2 %copy-done.2 = bf16[2,4096,512]{2,1,0:T(8,128)(2,1)} copy-done((bf16[2,4096,512]{2,1,0:T(8,128)(2,1)}, bf16[2,4096,512]{2,1,0:T(8,128)(2,1)S(1)}, u32[]{:S(2)}) %copy-start.2) | copy-done | bytes 8388632
  56.1 17.3 %pattern_steps.1 = (bf16[2,4096,512]{2,1,0:T(8,128)(2,1)}, f32[2,256,256]{2,1,0:T(8,128)}) custom-call(s32[6]{0:T(128)} %get-tuple-element.15.row_ref, s32[6]{0:T(128)} %get-tuple-element.14.col_ref, s32[1]{0:T(128)} %bitcast.9.live_ref, f32[2,256,256]{2,1,0:T(8,128)} %probe_ref.1, f32[6,256,256]{2,1,0:T(8,128)} %bitcast.12, ...), custom_call_target="tpu_custom_call", output_to_operand_aliasing={{0}: (16, {})} | custom-call | tf_op jit(solution)/shard_map/pattern_steps/pallas_call | solution.py:352
  73.4 0.0 copy-start.1
  73.4 3.4 %copy-done.1 = bf16[2,4096,512]{2,1,0:T(8,128)(2,1)S(1)} copy-done((bf16[2,4096,512]{2,1,0:T(8,128)(2,1)S(1)}, bf16[2,4096,512]{2,1,0:T(8,128)(2,1)}, u32[]{:S(2)}) %copy-start.1) | copy-done | bytes 8388632
  76.8 0.0 copy-start.3
  76.8 1.0 copy-done.3
  77.8 51.7 %reduce_steps.1 = (f32[2,256,512]{2,1,0:T(8,128)S(1)}, f32[2,8,2,16,256]{4,3,2,1,0:T(8,128)S(1)}) custom-call(bf16[2,4096,512]{2,1,0:T(8,128)(2,1)S(1)} %copy-done.1, f32[2,8,2,16,256]{4,3,2,1,0:T(8,128)S(1)} %bitcast.10), custom_call_target="tpu_custom_call" | custom-call | tf_op jit(solution)/shard_map/reduce_steps/pallas_call | solution.py:579
  129.5 1.0 copy.22
  130.5 0.8 copy.23
Async XLA Ops:
  49.7 3.2 %copy-start = (bf16[2,4096,512]{2,1,0:T(8,128)(2,1)}, bf16[2,4096,512]{2,1,0:T(8,128)(2,1)S(1)}, u32[]{:S(2)}) copy-start(bf16[2,4096,512]{2,1,0:T(8,128)(2,1)S(1)} %get-tuple-element.9.rest_9_) | copy-start | bytes 25165828
  52.9 3.2 %copy-start.2 = (bf16[2,4096,512]{2,1,0:T(8,128)(2,1)}, bf16[2,4096,512]{2,1,0:T(8,128)(2,1)S(1)}, u32[]{:S(2)}) copy-start(bf16[2,4096,512]{2,1,0:T(8,128)(2,1)S(1)} %get-tuple-element.8.rest_8_) | copy-start | bytes 25165828
  73.4 3.4 %copy-start.1 = (bf16[2,4096,512]{2,1,0:T(8,128)(2,1)S(1)}, bf16[2,4096,512]{2,1,0:T(8,128)(2,1)}, u32[]{:S(2)}) copy-start(bf16[2,4096,512]{2,1,0:T(8,128)(2,1)} %get-tuple-element.10.x_ref) | copy-start | bytes 25165828
  76.8 1.0 copy-start.3

commit v3 on v2

--- a/solution.py
+++ b/solution.py
@@ -11,6 +11,7 @@
 
 MESH = pl.DeviceIdType.MESH
 ANY = pl.BlockSpec(memory_space=pl.ANY)
+HBM = pl.BlockSpec(memory_space=pltpu.HBM)
 VMEM = pl.BlockSpec(memory_space=pltpu.VMEM)
 ROWS16 = 16
 
@@ -128,7 +129,7 @@
         functools.partial(gather_kernel, count),
         out_shape=(whole, whole),
         in_specs=[ANY],
-        out_specs=(ANY, ANY),
+        out_specs=(HBM, HBM),
         scratch_shapes=[
             pltpu.VMEM((planes, 2 * rows, columns), tile_low.dtype),
             dma((2, reach, 2)),
@@ -139,7 +140,7 @@
             dma((count // 2,)),
         ],
         compiler_params=pltpu.CompilerParams(
-            collective_id=0, has_side_effects=True, vmem_limit_bytes=16 * 2**20
+            collective_id=0, has_side_effects=True, vmem_limit_bytes=60 * 2**20
         ),
         name="gather_object",
     )(tile_low)
@@ -219,7 +220,7 @@
 
 
 def pattern_kernel(
-    row_ref, col_ref, live_ref, probe_ref, measured_ref, down_ref, across_ref, *rest,
+    place_ref, live_ref, probe_ref, measured_ref, down_ref, across_ref, *rest,
 ):
     tables, rest = rest[:8], rest[8:]
     (object_ref, blank_ref, steps_ref, sum_ref, windows, staged, in_sem, out_sem) = rest
@@ -232,7 +233,7 @@
     stripe = windows.shape[3]
 
     def aligned(index):
-        return pl.multiple_of(row_ref[index] // ROWS16 * ROWS16, ROWS16)
+        return pl.multiple_of(place_ref[index, 0] // ROWS16 * ROWS16, ROWS16)
 
     def fetch(index):
         return pltpu.make_async_copy(
@@ -255,15 +256,16 @@
     apart = lax.broadcasted_iota(jnp.int32, (stripe, pixels), 0) - lax.broadcasted_iota(
         jnp.int32, (stripe, pixels), 1
     )
+    column_base = lax.axis_index("obj") * stripe
     picks, patches, waves = [], [], []
     probe_real = probe_ref[0]
     probe_imag = probe_ref[1]
     for member in range(group):
         slot = turn * group + member
-        pick = jnp.where(apart == col_ref[slot], 1.0, 0.0).astype(jnp.bfloat16)
+        pick = jnp.where(apart == place_ref[slot, 1] - column_base, 1.0, 0.0).astype(jnp.bfloat16)
         both = jnp.concatenate([windows[slot, 0], windows[slot, 1]], axis=0)
         moved = jnp.dot(both, pick, preferred_element_type=jnp.float32)
-        shift = lax.rem(tall - lax.rem(row_ref[slot], ROWS16), tall)
+        shift = lax.rem(tall - lax.rem(place_ref[slot, 0], ROWS16), tall)
         object_real = pltpu.roll(moved[:tall], shift, 0)[:pixels]
         object_imag = pltpu.roll(moved[tall:], shift, 0)[:pixels]
         picks.append(pick)
@@ -291,7 +293,7 @@
         object_real, object_imag = patches[member]
         total_real += object_real * back_real + object_imag * back_imag
         total_imag += object_real * back_imag - object_imag * back_real
-        row_off = lax.rem(row_ref[slot], ROWS16)
+        row_off = lax.rem(place_ref[slot, 0], ROWS16)
 
         def shifted(value):
             low = value.astype(jnp.bfloat16).astype(jnp.float32)
@@ -341,7 +343,7 @@
     return tables
 
 
-def pattern_steps(whole, blank, probe_field, measured, rows, cols, live):
+def pattern_steps(whole, blank, probe_field, measured, places, live):
     slots, pixels, _ = measured.shape
     stripe = whole.shape[2]
     tall = pixels + ROWS16
@@ -357,20 +359,20 @@
             jax.ShapeDtypeStruct(probe_field.shape, jnp.float32),
         ),
         in_specs=[
-            smem, smem, smem, plane, pl.BlockSpec((group, pixels, pixels), lambda turn: (turn, 0, 0)),
-            *[pl.BlockSpec(table.shape, lambda turn: (0, 0)) for table in tables], ANY, ANY,
+            smem, smem, plane, pl.BlockSpec((group, pixels, pixels), lambda turn: (turn, 0, 0)),
+            *[pl.BlockSpec(table.shape, lambda turn: (0, 0)) for table in tables], HBM, HBM,
         ],
-        out_specs=(ANY, plane),
+        out_specs=(HBM, plane),
         scratch_shapes=[
             pltpu.VMEM((slots, 2, tall, stripe), jnp.bfloat16),
             pltpu.VMEM((slots, 2, tall, stripe), jnp.bfloat16),
             pltpu.SemaphoreType.DMA((slots,)),
             pltpu.SemaphoreType.DMA((slots,)),
         ],
-        input_output_aliases={6 + len(tables): 0},
+        input_output_aliases={5 + len(tables): 0},
         compiler_params=pltpu.CompilerParams(vmem_limit_bytes=60 * 2**20),
         name="pattern_steps",
-    )(rows, cols, live, probe_field, measured, *tables, whole, blank)
+    )(places, live, probe_field, measured, *tables, whole, blank)
 
 
 def reduce_kernel(
@@ -582,7 +584,7 @@
             jax.ShapeDtypeStruct((planes, rows, columns), jnp.float32),
             jax.ShapeDtypeStruct((2, pairs, 2, share, pixels), jnp.float32),
         ),
-        in_specs=[ANY, ANY],
+        in_specs=[HBM, HBM],
         out_specs=(VMEM, ANY),
         scratch_shapes=[
             pltpu.VMEM((pairs, 2, rows, columns), jnp.bfloat16),
@@ -609,7 +611,7 @@
             dma,
         ],
         compiler_params=pltpu.CompilerParams(
-            collective_id=1, has_side_effects=True, vmem_limit_bytes=40 * 2**20
+            collective_id=1, has_side_effects=True, vmem_limit_bytes=60 * 2**20
         ),
         name="reduce_steps",
     )(steps, probe_part.reshape(2, pairs, 2, share, pixels))
@@ -618,18 +620,15 @@
 
 def on_device(object_field, probe_field, intensities, positions, live_counts):
     pixels = probe_field.shape[1]
-    stripe = object_field.shape[2]
     slots = positions.shape[2]
     count = lax.axis_size("scan")
     whole, blank = gather_object(object_field.astype(jnp.bfloat16), count)
-    places = positions.reshape(slots, 2)
     steps, probe_part = pattern_steps(
         whole,
         blank,
         probe_field,
         intensities.reshape(slots, pixels, pixels),
-        places[:, 0],
-        places[:, 1] - lax.axis_index("obj") * stripe,
+        positions.reshape(slots, 2),
         live_counts.reshape(1),
     )
     object_grad, probe_grad = reduce_steps(steps, probe_part, count)

time: 134 us -> 129 us (0.963)
  local copies, waits for them, and re-layouts: 14 us -> 5.48 us
  Pallas kernels: 115 us -> 117 us
    unnamed x10 -> x2, local copies, waits for them, and re-layouts: 12.6 us -> 4.13 us
    pallas_call x1, Pallas kernels: 51.7 us -> 53.4 us  [reduce_steps(): pl.pallas_call(functools.partial(reduce_kernel, count), out_shape=(jax.Sh...]
    reshape x0 -> x1, local copies, waits for them, and re-layouts: none -> 1.35 us  [on_device(): positions.reshape(slots, 2)]
    squeeze x1 -> x0, local copies, waits for them, and re-layouts: 1.34 us -> none  [on_device(): places[:, 1] - lax.axis_index('obj') * stripe]
where the time goes in v3:
time: 129 us; the launch traced here: 126 us
  Pallas kernels  117 us (91%)
  local copies, waits for them, and re-layouts  5.48 us (4%)
  other arithmetic  2.08 us (2%)
  between operations  1.3 us (1%)
    pallas_call x1, Pallas kernels, reduce_steps(): pl.pallas_call(functools.partial(reduce_kernel, count), out_shape=(jax.Sh...  53.4 us
    pallas_call x1, Pallas kernels, gather_object(): pl.pallas_call(functools.partial(gather_kernel, count), out_shape=(whole,...  46.6 us
    pallas_call x1, Pallas kernels, pattern_steps(): pl.pallas_call(pattern_kernel, grid=(slots // group,), out_shape=(jax.Sha...  17.3 us
    unnamed x2, local copies, waits for them, and re-layouts  4.13 us

profile of v3, /device:TPU:15, one launch (start us, length us, event | category | flops | bytes accessed | tf_op | source)
XLA Modules:
  0.0 126.2 jit_solution(8830448009065669372)
XLA Ops:
  1.3 1.4 %copy.18.place_ref = s32[6,2]{1,0:T(8,128)} copy(s32[6,2]{0,1:T(2,128)} %bitcast.9) | data formatting | bytes 96 | tf_op jit(solution)/shard_map/reshape | solution.py:631
  2.6 2.1 %convert_element_type.3.x_ref = bf16[2,256,512]{2,1,0:T(8,128)(2,1)} convert(f32[2,256,512]{2,1,0:T(8,128)} %param.15) | non-fusion elementwise | flops 262144 | bytes 1572864 | tf_op jit(solution)/shard_map/convert_element_type | solution.py:625
  4.7 46.6 %gather_object.1 = (bf16[2,4096,512]{2,1,0:T(8,128)(2,1)}, bf16[2,4096,512]{2,1,0:T(8,128)(2,1)}) custom-call(bf16[2,256,512]{2,1,0:T(8,128)(2,1)} %convert_element_type.3.x_ref), custom_call_target="tpu_custom_call" | custom-call | tf_op jit(solution)/shard_map/gather_object/pallas_call | solution.py:128
  51.4 17.3 %pattern_steps.1 = (bf16[2,4096,512]{2,1,0:T(8,128)(2,1)}, f32[2,256,256]{2,1,0:T(8,128)}) custom-call(s32[6,2]{1,0:T(8,128)} %copy.18.place_ref, s32[1]{0:T(128)} %bitcast.5.live_ref, f32[2,256,256]{2,1,0:T(8,128)} %probe_ref.1, f32[6,256,256]{2,1,0:T(8,128)} %bitcast.6, ...), custom_call_target="tpu_custom_call", output_to_operand_aliasing={{0}: (15, {})} | custom-call | tf_op jit(solution)/shard_map/pattern_steps/pallas_call | solution.py:354
  68.7 53.4 %reduce_steps.1 = (f32[2,256,512]{2,1,0:T(8,128)}, f32[2,8,2,16,256]{4,3,2,1,0:T(8,128)}) custom-call(bf16[2,4096,512]{2,1,0:T(8,128)(2,1)} %get-tuple-element.10.x_ref, f32[2,8,2,16,256]{4,3,2,1,0:T(8,128)} %bitcast.7), custom_call_target="tpu_custom_call" | custom-call | tf_op jit(solution)/shard_map/reduce_steps/pallas_call | solution.py:581
  122.1 2.3 %copy.23 = f32[2,256,512]{2,1,0:T(8,128)} copy(f32[2,256,512]{2,1,0:T(8,128)} %get-tuple-element.16) | data formatting | bytes 2097152
  124.3 1.9 %copy.24 = f32[2,256,256]{2,1,0:T(8,128)} copy(f32[2,256,256]{2,1,0:T(8,128)} %bitcast.8) | data formatting | bytes 1048576

commit v4 on v3

--- a/solution.py
+++ b/solution.py
@@ -140,7 +140,7 @@
             dma((count // 2,)),
         ],
         compiler_params=pltpu.CompilerParams(
-            collective_id=0, has_side_effects=True, vmem_limit_bytes=60 * 2**20
+            collective_id=0, has_side_effects=True, vmem_limit_bytes=16 * 2**20
         ),
         name="gather_object",
     )(tile_low)
@@ -611,7 +611,7 @@
             dma,
         ],
         compiler_params=pltpu.CompilerParams(
-            collective_id=1, has_side_effects=True, vmem_limit_bytes=60 * 2**20
+            collective_id=1, has_side_effects=True, vmem_limit_bytes=24 * 2**20
         ),
         name="reduce_steps",
     )(steps, probe_part.reshape(2, pairs, 2, share, pixels))

time: 129 us -> 134 us (1.039)
  local copies, waits for them, and re-layouts: 5.48 us -> 14 us
  Pallas kernels: 117 us -> 115 us
    unnamed x2 -> x10, local copies, waits for them, and re-layouts: 4.13 us -> 12.6 us
    pallas_call x1, Pallas kernels: 53.4 us -> 51.7 us  [reduce_steps(): pl.pallas_call(functools.partial(reduce_kernel, count), out_shape=(jax.Sh...]
where the time goes in v4:
time: 134 us; the launch traced here: 131 us
  Pallas kernels  115 us (86%)
  local copies, waits for them, and re-layouts  14 us (10%)
    pallas_call x1, Pallas kernels, reduce_steps(): pl.pallas_call(functools.partial(reduce_kernel, count), out_shape=(jax.Sh...  51.7 us
    pallas_call x1, Pallas kernels, gather_object(): pl.pallas_call(functools.partial(gather_kernel, count), out_shape=(whole,...  45.8 us
    pallas_call x1, Pallas kernels, pattern_steps(): pl.pallas_call(pattern_kernel, grid=(slots // group,), out_shape=(jax.Sha...  17.2 us
    unnamed x10, local copies, waits for them, and re-layouts  12.6 us

profile of v4, /device:TPU:15, one launch (start us, length us, event | category | flops | bytes accessed | tf_op | source)
XLA Modules:
  0.0 131.3 jit_solution(12293003138423372528)
XLA Ops:
  1.3 1.4 %copy.18.place_ref = s32[6,2]{1,0:T(8,128)} copy(s32[6,2]{0,1:T(2,128)} %bitcast.9) | data formatting | bytes 96 | tf_op jit(solution)/shard_map/reshape | solution.py:631
  2.6 1.3 convert_element_type.3.x_ref
  3.9 45.8 %gather_object.1 = (bf16[2,4096,512]{2,1,0:T(8,128)(2,1)S(1)}, bf16[2,4096,512]{2,1,0:T(8,128)(2,1)S(1)}) custom-call(bf16[2,256,512]{2,1,0:T(8,128)(2,1)S(1)} %convert_element_type.3.x_ref), custom_call_target="tpu_custom_call" | custom-call | tf_op jit(solution)/shard_map/gather_object/pallas_call | solution.py:128
  49.7 0.0 copy-start
  49.7 3.2 %copy-done = bf16[2,4096,512]{2,1,0:T(8,128)(2,1)} copy-done((bf16[2,4096,512]{2,1,0:T(8,128)(2,1)}, bf16[2,4096,512]{2,1,0:T(8,128)(2,1)S(1)}, u32[]{:S(2)}) %copy-start) | copy-done | bytes 8388632
  52.9 0.0 copy-start.2
  52.9 3.2 %copy-done.2 = bf16[2,4096,512]{2,1,0:T(8,128)(2,1)} copy-done((bf16[2,4096,512]{2,1,0:T(8,128)(2,1)}, bf16[2,4096,512]{2,1,0:T(8,128)(2,1)S(1)}, u32[]{:S(2)}) %copy-start.2) | copy-done | bytes 8388632
  56.1 17.2 %pattern_steps.1 = (bf16[2,4096,512]{2,1,0:T(8,128)(2,1)}, f32[2,256,256]{2,1,0:T(8,128)}) custom-call(s32[6,2]{1,0:T(8,128)} %copy.18.place_ref, s32[1]{0:T(128)} %bitcast.5.live_ref, f32[2,256,256]{2,1,0:T(8,128)} %probe_ref.1, f32[6,256,256]{2,1,0:T(8,128)} %bitcast.8, ...), custom_call_target="tpu_custom_call", output_to_operand_aliasing={{0}: (15, {})} | custom-call | tf_op jit(solution)/shard_map/pattern_steps/pallas_call | solution.py:354
  73.4 0.0 copy-start.1
  73.4 3.4 %copy-done.1 = bf16[2,4096,512]{2,1,0:T(8,128)(2,1)S(1)} copy-done((bf16[2,4096,512]{2,1,0:T(8,128)(2,1)S(1)}, bf16[2,4096,512]{2,1,0:T(8,128)(2,1)}, u32[]{:S(2)}) %copy-start.1) | copy-done | bytes 8388632
  76.8 0.0 copy-start.3
  76.8 1.0 copy-done.3
  77.8 51.7 %reduce_steps.1 = (f32[2,256,512]{2,1,0:T(8,128)S(1)}, f32[2,8,2,16,256]{4,3,2,1,0:T(8,128)S(1)}) custom-call(bf16[2,4096,512]{2,1,0:T(8,128)(2,1)S(1)} %copy-done.1, f32[2,8,2,16,256]{4,3,2,1,0:T(8,128)S(1)} %bitcast.6), custom_call_target="tpu_custom_call" | custom-call | tf_op jit(solution)/shard_map/reduce_steps/pallas_call | solution.py:581
  129.5 1.0 copy.23
  130.5 0.8 copy.24
Async XLA Ops:
  49.7 3.2 %copy-start = (bf16[2,4096,512]{2,1,0:T(8,128)(2,1)}, bf16[2,4096,512]{2,1,0:T(8,128)(2,1)S(1)}, u32[]{:S(2)}) copy-start(bf16[2,4096,512]{2,1,0:T(8,128)(2,1)S(1)} %get-tuple-element.9.rest_9_) | copy-start | bytes 25165828
  52.9 3.2 %copy-start.2 = (bf16[2,4096,512]{2,1,0:T(8,128)(2,1)}, bf16[2,4096,512]{2,1,0:T(8,128)(2,1)S(1)}, u32[]{:S(2)}) copy-start(bf16[2,4096,512]{2,1,0:T(8,128)(2,1)S(1)} %get-tuple-element.8.rest_8_) | copy-start | bytes 25165828
  73.4 3.4 %copy-start.1 = (bf16[2,4096,512]{2,1,0:T(8,128)(2,1)S(1)}, bf16[2,4096,512]{2,1,0:T(8,128)(2,1)}, u32[]{:S(2)}) copy-start(bf16[2,4096,512]{2,1,0:T(8,128)(2,1)} %get-tuple-element.10.x_ref) | copy-start | bytes 25165828
  76.8 1.0 copy-start.3
